TPU v7x, 128 devices: a whole 4x4x4 slice. The times are simulated.
128 devices in a mesh: tm: 16 (over y_hi, z, core), space: 8 (over x, y_lo).
Axes of the slice: x: 4, y: 4 (y_hi: 2, y_lo: 2; y = y_hi * 2 + y_lo), z: 4, core: 2. Of those that a mesh axis runs over, the one named last changes fastest.
Arguments:
- query: bfloat16 [32, 2048, 3072], P('tm', 'space'), may hold values from -204 to 204
- key_proj: bfloat16 [32, 2048, 3072], P('tm', 'space'), may hold values from -6 to 6
- value: bfloat16 [32, 2048, 3072], P('tm', 'space'), may hold values from -6 to 6
- head_class: int32 [24], replicated, may hold values from 0 to 1, as said below
- frame_count: int32 [1], replicated, may hold values from 24 to 31
Outputs:
- attended: bfloat16 [32, 2048, 3072], P('tm', 'space')
Inputs may be any that keep to these rules, and one draw needn't show every extreme that they name: `head_class`: exactly 8 of the 24 heads are temporal, the others spatial. Frames of index frame_count[0] or more are padding.
All inputs are finite; a program needn't handle non-finite values.
Results may differ from a plain program's by a relative error of at most 0.0085.
Values may be sent and summed in bfloat16 or wider, within the bound.
A program may use at most 320 MiB of HBM per device.

v0:
```python
import math

import jax
import jax.numpy as jnp
from jax import lax
from jax.sharding import PartitionSpec as P

HEADS = 24
TEMP_HEADS = 8


NEG_FILL = -1e30


def frame_attend(parts):
    queries, key_rows, value_rows = parts
    item_count, length, head_count, head_depth = queries.shape
    scale = head_depth ** (-0.5)
    block_rows = math.gcd(length, 512)
    values_wide = value_rows.astype(jnp.float32)
    blocked = queries.reshape(
        item_count, length // block_rows, block_rows, head_count, head_depth
    ).transpose(1, 0, 2, 3, 4)

    def one_block(query_block):
        scores = (
            jnp.einsum("nqhd,nkhd->nhqk", query_block, key_rows, preferred_element_type=jnp.float32)
            * scale
        )
        weights = jnp.exp(scores - jnp.max(scores, axis=-1, keepdims=True))
        totals = jnp.sum(weights, axis=-1, keepdims=True)
        mixed = jnp.einsum("nhqk,nkhd->nqhd", weights, values_wide)
        return mixed / jnp.transpose(totals, (0, 2, 1, 3))

    results = lax.map(one_block, blocked)
    return (
        results.transpose(1, 0, 2, 3, 4)
        .reshape(item_count, length, head_count, head_depth)
        .astype(jnp.bfloat16)
    )


def temporal_folded(query_time, keys_time, values_time, frame_limit):
    frames_dev, pos_dev, head_count, head_depth = query_time.shape
    scale = head_depth ** (-0.5)
    peak = jnp.full((frames_dev, pos_dev, head_count), NEG_FILL, jnp.float32)
    key_piece = lax.all_gather(keys_time, "tm", axis=0, tiled=True)
    value_piece = lax.all_gather(values_time, "tm", axis=0, tiled=True)
    scores = (
        jnp.einsum("fphd,gphd->fphg", query_time, key_piece, preferred_element_type=jnp.float32)
        * scale
    )
    valid = jnp.arange(key_piece.shape[0], dtype=jnp.int32) < frame_limit
    scores = jnp.where(valid, scores, -jnp.inf)
    new_peak = jnp.maximum(peak, jnp.max(scores, axis=-1))
    weights = jnp.exp(scores - new_peak[..., None])
    total = jnp.sum(weights, axis=-1)
    summed = jnp.einsum("fphg,gphd->fphd", weights, value_piece.astype(jnp.float32))
    peak, total, summed = (new_peak, total, summed)
    return (summed / total[..., None]).astype(jnp.bfloat16)


def on_device(query, key_proj, value, head_class, frame_count):
    frames_dev, pos_dev, width = query.shape
    space_heads = HEADS - TEMP_HEADS
    head_order = jnp.argsort(head_class, stable=True)
    inverse = jnp.argsort(head_order, stable=True)
    frame_limit = frame_count[0]

    def select(array, chosen):
        return jnp.take(array.reshape(frames_dev, pos_dev, HEADS, width // HEADS), chosen, axis=2)

    spatial_heads = head_order[:space_heads]
    temporal_heads = head_order[space_heads:]
    query_space = select(query, spatial_heads)
    keys_space = select(key_proj, spatial_heads)
    values_space = select(value, spatial_heads)
    query_time = select(query, temporal_heads)
    keys_time = select(key_proj, temporal_heads)
    values_time = select(value, temporal_heads)
    spatial_out = lax.all_to_all(
        frame_attend(
            (
                lax.all_to_all(query_space, "space", split_axis=2, concat_axis=1, tiled=True),
                lax.all_to_all(keys_space, "space", split_axis=2, concat_axis=1, tiled=True),
                lax.all_to_all(values_space, "space", split_axis=2, concat_axis=1, tiled=True),
            )
        ),
        "space",
        split_axis=1,
        concat_axis=2,
        tiled=True,
    )
    temporal_out = temporal_folded(query_time, keys_time, values_time, frame_limit)
    joined = jnp.concatenate([spatial_out, temporal_out], axis=2)
    restored = jnp.take(joined, inverse, axis=2)
    frame_ids = lax.axis_index("tm") * frames_dev + jnp.arange(frames_dev, dtype=jnp.int32)
    restored = jnp.where(
        (frame_ids < frame_limit)[:, None, None, None], restored, jnp.zeros_like(restored)
    )
    return restored.reshape(frames_dev, pos_dev, width)


def solution(mesh):
    return jax.shard_map(
        on_device,
        mesh=mesh,
        in_specs=(P("tm", "space", None), P("tm", "space", None), P("tm", "space", None), P(), P()),
        out_specs=P("tm", "space", None),
        check_vma=False,
    )
```

profile of v0, /device:TPU:1, one launch (start us, length us, event | category | flops | bytes accessed | tf_op | source)
XLA Modules:
  0.0 387.3 jit_solution(9464426233776752746)
XLA Ops:
  8.9 4.6 %copy.120 = bf16[2,256,3072]{1,2,0:T(8,128)(2,1)} copy(bf16[2,256,3072]{2,1,0:T(8,128)(2,1)} %param.11) | data formatting | bytes 6291456 | tf_op args[0]
  13.5 3.5 copy.121
  17.0 4.6 %copy.123 = bf16[2,256,3072]{1,2,0:T(8,128)(2,1)} copy(bf16[2,256,3072]{2,1,0:T(8,128)(2,1)} %param.12) | data formatting | bytes 6291456 | tf_op args[1]
  21.6 4.7 %copy.124 = bf16[2,256,24,128]{3,1,2,0:T(8,128)(2,1)} copy(bf16[2,256,24,128]{1,3,2,0:T(8,128)(2,1)} %bitcast.101) | data formatting | bytes 6291456 | tf_op jit(solution)/shard_map/reshape | solution.py:71
  28.0 3.6 gather_fusion.5
  31.5 4.6 %copy.127 = bf16[2,256,3072]{1,2,0:T(8,128)(2,1)} copy(bf16[2,256,3072]{2,1,0:T(8,128)(2,1)} %param.13) | data formatting | bytes 6291456 | tf_op args[2]
  36.2 4.6 %copy.128 = bf16[2,256,24,128]{3,1,2,0:T(8,128)(2,1)} copy(bf16[2,256,24,128]{1,3,2,0:T(8,128)(2,1)} %bitcast.102) | data formatting | bytes 6291456 | tf_op jit(solution)/shard_map/reshape | solution.py:71
  40.8 3.5 gather_fusion.4
  44.3 3.5 select_bitcast_fusion.3
  54.6 4.2 %gather_fusion.2 = bf16[16,2,256,128]{3,2,1,0:T(8,128)(2,1)} fusion(bf16[2,256,24,128]{3,1,2,0:T(8,128)(2,1)} %copy.124, s32[1024]{0:T(1024)S(1)} %pad_clamp_fusion.2), kind=kCustom, calls=%fused_computation.2.clone | custom fusion | bytes 4194368 | tf_op jit(solution)/shard_map/jit(_take)/gather | solution.py:71
  61.0 5.4 %select_bitcast_fusion = (bf16[2,256,16,128]{3,1,0,2:T(8,128)(2,1)S(1)}, bf16[2,256,16,128]{3,1,0,2:T(8,128)(2,1)S(1)}, bf16[2,256,16,128]{3,1,0,2:T(8,128)(2,1)}) fusion(bf16[16,2,256,128]{3,2,1,0:T(8,128)(2,1)} %gather_fusion.3, pred[16]{0:T(512)(128)(4,1)S(1)} %get-tuple-element.79, bf16[16,2,256,128]{3,2,1,0:T(8,128)(2,1)} %gather_fusion.2, ...), kind=kLoop, calls=%fused_computation.34 | loop fusion | flops 3145728 | bytes 12582928 | tf_op jit(solution)/shard_map/jit(_take)/select_n | solution.py:71
  66.4 33.0 %all_to_all.60 = bf16[2,256,16,128]{3,1,0,2:T(8,128)(2,1)S(1)} all-to-all(bf16[2,256,16,128]{3,1,0,2:T(8,128)(2,1)S(1)} %get-tuple-element.85), channel_id=1, replica_groups=mesh['tm'=16,'space'=8] {'space'}, dimensions={2} | all-to-all | bytes 4194304 | tf_op jit(solution)/shard_map/all_to_all | solution.py:86
  99.4 30.2 %all_to_all.61 = bf16[2,256,16,128]{3,1,0,2:T(8,128)(2,1)} all-to-all(bf16[2,256,16,128]{3,1,0,2:T(8,128)(2,1)S(1)} %get-tuple-element.86), channel_id=1, replica_groups=mesh['tm'=16,'space'=8] {'space'}, dimensions={2} | all-to-all | bytes 4194304 | tf_op jit(solution)/shard_map/all_to_all | solution.py:85
  129.6 6.7 %all-to-all-start = ((bf16[2,256,16,128]{3,1,0,2:T(8,128)(2,1)}), bf16[2,256,16,128]{3,1,0,2:T(8,128)(2,1)}, u32[]{:S(2)}, u32[]{:S(2)}) async-start(bf16[2,256,16,128]{3,1,0,2:T(8,128)(2,1)} %get-tuple-element.87), calls=%async_computation | async-start | bytes 4194304 | tf_op jit(solution)/shard_map/all_to_all | solution.py:84
  138.8 27.9 %all-to-all-done = bf16[2,256,16,128]{3,1,0,2:T(8,128)(2,1)} async-done(((bf16[2,256,16,128]{3,1,0,2:T(8,128)(2,1)}), bf16[2,256,16,128]{3,1,0,2:T(8,128)(2,1)}, u32[]{:S(2)}, u32[]{:S(2)}) %all-to-all-start) | async-done | bytes 2097184 | tf_op jit(solution)/shard_map/all_to_all | solution.py:84
  169.9 47.1 %while.10 = (s32[]{:T(128)}, bf16[4,2,512,2,128]{4,2,0,3,1:T(8,128)(2,1)}, bf16[4,2,512,2,128]{4,2,0,3,1:T(8,128)(2,1)}, bf16[2,2048,2,128]{3,1,2,0:T(8,128)(2,1...) while((s32[]{:T(128)}, bf16[4,2,512,2,128]{4,2,0,3,1:T(8,128)(2,1)}, ...), condition=%wide.region_5.7_spmd, body=%wide.region_2.6_spmd.sunk | while | flops 2177101824 | bytes 81305760 | solution.py:35
  169.9 3.5 multiply_reduce_fusion.2
  176.7 3.6 fusion.35
  181.7 3.5 multiply_reduce_fusion.2
  188.5 3.6 fusion.35
  193.4 3.5 multiply_reduce_fusion.2
  200.2 3.6 fusion.35
  205.2 3.5 multiply_reduce_fusion.2
  212.0 3.6 fusion.35
  217.0 5.8 %copy.133 = bf16[2,2048,2,128]{3,2,0,1:T(2,128)(2,1)} copy(bf16[2,2048,2,128]{3,1,2,0:T(8,128)(2,1)} %bitcast.109) | data formatting | bytes 4194304 | tf_op jit(solution)/shard_map/convert_element_type | solution.py:39
  222.7 4.7 %all-to-all-start.3 = ((bf16[2,2048,2,128]{3,2,0,1:T(2,128)(2,1)}), bf16[2,2048,2,128]{3,2,0,1:T(2,128)(2,1)S(1)}, u32[]{:S(2)}, u32[]{:S(2)}) async-start(bf16[2,2048,2,128]{3,2,0,1:T(2,128)(2,1)} %copy.133), calls=%async_computation.3 | async-start | bytes 4194304 | tf_op jit(solution)/shard_map/all_to_all | solution.py:81
  229.9 27.8 %all-to-all-done.3 = bf16[2,2048,2,128]{3,2,0,1:T(2,128)(2,1)S(1)} async-done(((bf16[2,2048,2,128]{3,2,0,1:T(2,128)(2,1)}), bf16[2,2048,2,128]{3,2,0,1:T(2,128)(2,1)S(1)}, u32[]{:S(2)}, u32[]{:S(2)}) %all-to-all-start.3) | async-done | bytes 2097184 | tf_op jit(solution)/shard_map/all_to_all | solution.py:81
  259.6 19.3 %bitcast_reduce_fusion = (f32[2,256,8]{0,2,1:T(8,128)S(1)}, f32[256,8,32,2]{2,3,1,0:T(2,128)S(1)}) fusion(bf16[2,256,8,128]{3,1,0,2:T(8,128)(2,1)S(1)} %copy-done.7, bf16[32,256,8,128]{3,2,1,0:T(8,128)(2,1)} %all-gather.5.cloned.1.call-done, pred[32]{0:T(512)(128)(4,1)S(1)} %iota_compare_fusion), kind=kOutput, calls=%fused_computation.32 | convolution fusion | flops 33943552 | bytes 18366496 | tf_op jit(solution)/shard_map/fphd,gphd->fphg/dot_general | solution.py:50
  280.2 29.1 %fusion.22 = f32[2,256,8]{0,2,1:T(8,128)S(1)} fusion(f32[256,8,32,2]{2,3,1,0:T(2,128)S(1)} %get-tuple-element.92, f32[2,256,8]{0,2,1:T(8,128)S(1)} %broadcast_maximum_fusion), kind=kLoop, calls=%fused_computation.38 | loop fusion | flops 258048 | bytes 557056 | tf_op jit(solution)/shard_map/reduce_sum | solution.py:57
  311.0 37.2 %all-gather.3.cloned.1.call-done = bf16[32,256,8,128]{3,2,1,0:T(8,128)(2,1)} async-done(((bf16[2,256,8,128]{3,2,1,0:T(8,128)(2,1)}), bf16[32,256,8,128]{3,2,1,0:T(8,128)(2,1)}) %all-gather.3.cloned.1.call-update) | async-done | bytes 16777232 | tf_op jit(solution)/shard_map/all_gather | solution.py:48
  348.2 16.8 %fusion.13 = f32[256,8,128,2]{2,3,1,0:T(2,128)S(1)} fusion(bf16[32,256,8,128]{3,2,1,0:T(8,128)(2,1)} %all-gather.3.cloned.1.call-done, f32[256,8,32,2]{2,3,1,0:T(2,128)} %copy-done.6, f32[2,256,8]{0,2,1:T(8,128)S(1)} %broadcast_maximum_fusion), kind=kOutput, calls=%fused_computation.22 | convolution fusion | flops 33685504 | bytes 19415040 | tf_op jit(solution)/shard_map/fphg,gphd->fphd/dot_general | solution.py:58
  375.8 4.6 %copy.148 = bf16[2,256,3072]{2,1,0:T(8,128)(2,1)} copy(bf16[2,256,3072]{1,2,0:T(8,128)(2,1)} %fusion.17) | data formatting | bytes 6291456 | tf_op jit(solution)/shard_map/jit(_where)/select_n | solution.py:98
  (76 shorter events, 54.4 us)
Async XLA Ops:
  6.5 252.9 %all-gather.5.cloned.1.call-start = ((), (), s32[]{:S(2)}) async-start(), calls=%async_computation.5 | async-start | bytes 17825792 | tf_op jit(solution)/shard_map/all_gather | solution.py:47
  49.5 298.7 %all-gather.3.cloned.1.call-start = ((), (), s32[]{:S(2)}) async-start(), calls=%async_computation.4 | async-start | bytes 17825792 | tf_op jit(solution)/shard_map/all_gather | solution.py:48
  54.6 4.2 %copy-start = (bf16[2,256,24,128]{3,1,2,0:T(8,128)(2,1)S(1)}, bf16[2,256,24,128]{3,1,2,0:T(8,128)(2,1)}, u32[]{:S(2)}) copy-start(bf16[2,256,24,128]{3,1,2,0:T(8,128)(2,1)} %copy.128) | copy-start | bytes 9437188
  129.6 37.2 %all-to-all-start = ((bf16[2,256,16,128]{3,1,0,2:T(8,128)(2,1)}), bf16[2,256,16,128]{3,1,0,2:T(8,128)(2,1)}, u32[]{:S(2)}, u32[]{:S(2)}) async-start(bf16[2,256,16,128]{3,1,0,2:T(8,128)(2,1)} %get-tuple-element.87), calls=%async_computation | async-start | bytes 4194304 | tf_op jit(solution)/shard_map/all_to_all | solution.py:84
  136.3 2.3 copy-start.2
  173.4 3.3 copy-start.3
  173.4 3.3 copy-start.4
  180.4 1.3 copy-start.5
  185.1 3.3 copy-start.3
  185.1 3.3 copy-start.4
  192.1 1.3 copy-start.5
  196.9 3.3 copy-start.3
  196.9 3.3 copy-start.4
  203.9 1.3 copy-start.5
  208.7 3.3 copy-start.3
  208.7 3.3 copy-start.4
  215.7 1.3 copy-start.5
  222.7 34.9 %all-to-all-start.3 = ((bf16[2,2048,2,128]{3,2,0,1:T(2,128)(2,1)}), bf16[2,2048,2,128]{3,2,0,1:T(2,128)(2,1)S(1)}, u32[]{:S(2)}, u32[]{:S(2)}) async-start(bf16[2,2048,2,128]{3,2,0,1:T(2,128)(2,1)} %copy.133), calls=%async_computation.3 | async-start | bytes 4194304 | tf_op jit(solution)/shard_map/all_to_all | solution.py:81
  257.9 1.6 copy-start.7
  278.9 1.3 copy-start.6
  365.0 1.6 copy-start.1
Sparse Core Ops, SparseCore 0:
  49.6 166.3 all-gather.4
  218.5 129.6 all-gather.2
where the time goes:
time: 389 us; the launch traced here: 387 us
  waiting for transfers between devices  92.9 us (24%)
  local copies, waits for them, and re-layouts  81.5 us (21%)
  matrix products  64.5 us (17%)
  blocking collectives  63.1 us (16%)
  other arithmetic  59.3 us (15%)
  between operations  14.2 us (4%)
  starting transfers between devices  11.5 us (3%)
    all_gather x1, waiting for transfers between devices, temporal_folded(): value_piece = lax.all_gather(values_time, 'tm', axis=0, tiled=True)  37.2 us
    all_to_all x1, blocking collectives, on_device(): lax.all_to_all(values_space, 'space', split_axis=2, concat_axis=1, tiled=...  33 us
    all_to_all x1, blocking collectives, on_device(): lax.all_to_all(keys_space, 'space', split_axis=2, concat_axis=1, tiled=True)  30.2 us
    reduce_sum x1, other arithmetic, temporal_folded(): total = jnp.sum(weights, axis=-1)  29.1 us
    all_to_all x1, waiting for transfers between devices, on_device(): lax.all_to_all(query_space, 'space', split_axis=2, concat_axis=1, tiled=T...  27.9 us
    all_to_all x1, waiting for transfers between devices, on_device(): lax.all_to_all(frame_attend((lax.all_to_all(query_space, 'space', split_a...  27.8 us
    dot_general x1, matrix products, temporal_folded(): jnp.einsum('fphd,gphd->fphg', query_time, key_piece, preferred_element_ty...  19.3 us
    gather x6, local copies, waits for them, and re-layouts, select(): jnp.take(array.reshape(frames_dev, pos_dev, HEADS, width // HEADS), chose...  17.2 us
  transfers between devices with their start and end apart: 4, of which 3 were waited for; matrix products, arithmetic and copies ran while one was open for 32% of the time, Pallas kernels for 0%

commit v1 on v0

v1 whole, which is shorter than its diff:
```python
import functools

import jax
import jax.numpy as jnp
from jax import lax
from jax.experimental import pallas as pl
from jax.experimental.pallas import tpu as pltpu
from jax.sharding import PartitionSpec as P

HEADS = 24
TEMP_HEADS = 8
SPACE_HEADS = HEADS - TEMP_HEADS
HD = 128
FR = 2
ROWS = 256
TM = 16
SPACE = 8
UNITS = 4
HALF = ROWS // 2
GROUP = 16
LOG2E = 1.4426950408889634
EXP_SCALE = HD**-0.5 * LOG2E
MASKED = -1e30
MESH = pl.DeviceIdType.MESH
CONTRACT_LAST = (((1,), (1,)), ((), ()))


def softmax_parts(scores):
    peak = jnp.max(scores, axis=-1, keepdims=True)
    weights = jnp.exp2((scores - peak) * EXP_SCALE)
    return weights.astype(jnp.bfloat16), jnp.sum(weights, axis=-1, keepdims=True)


def attend_kernel(
    order_ref, count_ref, q_ref, k_ref, v_ref, r_ref,
    stage, recv, t_stage, t_recv, out_stage, t_out,
    fwd_send, fwd_recv, t_send, t_recv_sem, back_send, back_recv, tb_send, tb_recv, local_sem, t_local_sem,
):
    tm = lax.axis_index("tm")
    space = lax.axis_index("space")
    tensors = (q_ref, k_ref, v_ref)

    def space_peer(step):
        return lax.rem(space // 2 + step // 2, 4) * 2 + lax.rem(space + step, 2)

    def tm_peer(step):
        high = lax.rem(tm // 8 + step // 8, 2)
        depth = lax.rem(tm // 2 + step // 2, 4)
        return (high * 4 + depth) * 2 + lax.rem(tm + step, 2)

    def fwd_copy(unit, peer, slot):
        return pltpu.make_async_remote_copy(
            src_ref=stage.at[unit, peer], dst_ref=recv.at[unit, slot],
            send_sem=fwd_send.at[unit, peer], recv_sem=fwd_recv.at[unit, slot],
            device_id=(tm, peer), device_id_type=MESH,
        )

    def back_copy(unit, peer, owner):
        return pltpu.make_async_remote_copy(
            src_ref=out_stage.at[unit, peer],
            dst_ref=r_ref.at[2 * owner + unit // 2, lax.rem(unit, 2)],
            send_sem=back_send.at[unit, peer], recv_sem=back_recv.at[unit, owner],
            device_id=(tm, peer), device_id_type=MESH,
        )

    def t_copy(peer, slot):
        return pltpu.make_async_remote_copy(
            src_ref=t_stage.at[peer], dst_ref=t_recv.at[slot],
            send_sem=t_send.at[peer], recv_sem=t_recv_sem.at[slot],
            device_id=(peer, space), device_id_type=MESH,
        )

    def t_back_copy(peer, owner):
        return pltpu.make_async_remote_copy(
            src_ref=t_out.at[peer],
            dst_ref=r_ref.at[SPACE_HEADS + owner // 2, :, pl.ds(HALF * lax.rem(owner, 2), HALF)],
            send_sem=tb_send.at[peer], recv_sem=tb_recv.at[owner],
            device_id=(peer, space), device_id_type=MESH,
        )

    barrier = pltpu.get_barrier_semaphore()

    def greet_space(step, carry):
        pl.semaphore_signal(barrier, inc=1, device_id=(tm, space_peer(step)), device_id_type=MESH)
        return carry

    def greet_tm(step, carry):
        pl.semaphore_signal(barrier, inc=1, device_id=(tm_peer(step), space), device_id_type=MESH)
        return carry

    lax.fori_loop(1, SPACE, greet_space, 0)
    lax.fori_loop(1, TM, greet_tm, 0)

    def stage_unit(unit):
        frame = lax.rem(unit, 2)

        def one(step, carry):
            peer = space_peer(step)
            head = order_ref[2 * peer + unit // 2]
            lanes = pl.ds(head * HD, HD)
            for index, tensor in enumerate(tensors):
                stage[unit, peer, index] = tensor[frame, :, lanes]
            return carry

        lax.fori_loop(0, SPACE, one, 0)

    def send_unit(unit):
        def one(step, carry):
            peer = space_peer(step)
            fwd_copy(unit, peer, space).start()
            return carry

        lax.fori_loop(1, SPACE, one, 0)
        recv[unit, space] = stage[unit, space]

    def stage_temporal():
        def one(step, carry):
            head = order_ref[SPACE_HEADS + step]
            lanes = pl.ds(head * HD, HD)
            for index, tensor in enumerate(tensors):
                for half in range(2):
                    t_stage[2 * step + half, index] = tensor[:, half * HALF:(half + 1) * HALF, lanes]
            return carry

        lax.fori_loop(0, TEMP_HEADS, one, 0)

    def send_temporal():
        def one(step, carry):
            t_copy(tm_peer(step), tm).start()
            return carry

        lax.fori_loop(1, TM, one, 0)
        t_recv[tm] = t_stage[tm]

    stage_unit(0)
    pl.semaphore_wait(barrier, SPACE + TM - 2)
    send_unit(0)
    stage_temporal()
    send_temporal()

    def later_unit(unit, carry):
        stage_unit(unit)
        send_unit(unit)
        return carry

    lax.fori_loop(1, UNITS, later_unit, 0)

    def attend_unit(unit):
        def arrived(step, carry):
            peer = space_peer(step)
            fwd_copy(unit, peer, peer).wait_recv()
            return carry

        lax.fori_loop(1, SPACE, arrived, 0)

        def block(step, carry):
            peer = space_peer(lax.rem(step + 1, SPACE))
            keys = recv[unit, :, 1].reshape(SPACE * ROWS, HD)
            values = recv[unit, :, 2].reshape(SPACE * ROWS, HD)
            scores = lax.dot_general(
                recv[unit, peer, 0], keys, CONTRACT_LAST, preferred_element_type=jnp.float32
            )
            weights, total = softmax_parts(scores)
            mixed = jnp.dot(weights, values, preferred_element_type=jnp.float32)
            out_stage[unit, peer] = (mixed / total).astype(jnp.bfloat16)

            @pl.when(step < SPACE - 1)
            def _():
                back_copy(unit, peer, space).start()

            return carry

        lax.fori_loop(0, SPACE, block, 0)
        pltpu.make_async_copy(
            out_stage.at[unit, space], r_ref.at[2 * space + unit // 2, lax.rem(unit, 2)], local_sem.at[unit]
        ).start()

    def attend_temporal():
        def arrived(step, carry):
            peer = tm_peer(step)
            t_copy(peer, peer).wait_recv()
            return carry

        lax.fori_loop(1, TM, arrived, 0)
        width = TM * FR * GROUP
        row = lax.broadcasted_iota(jnp.int32, (width, width), 0)
        column = lax.broadcasted_iota(jnp.int32, (width, width), 1)
        same = (row % GROUP) == (column % GROUP)
        allowed = same & (column < count_ref[0] * GROUP)

        def group(index, carry):
            span = pl.ds(pl.multiple_of(index * GROUP, GROUP), GROUP)
            queries = t_recv[:, 0, :, span].reshape(width, HD)
            keys = t_recv[:, 1, :, span].reshape(width, HD)
            values = t_recv[:, 2, :, span].reshape(width, HD)
            scores = lax.dot_general(queries, keys, CONTRACT_LAST, preferred_element_type=jnp.float32)
            weights, total = softmax_parts(jnp.where(allowed, scores, MASKED))
            mixed = jnp.dot(weights, values, preferred_element_type=jnp.float32)
            t_out[:, :, span] = (mixed / total).astype(jnp.bfloat16).reshape(TM, FR, GROUP, HD)
            return carry

        lax.fori_loop(0, HALF // GROUP, group, 0)

        def back(step, carry):
            t_back_copy(tm_peer(step), tm).start()
            return carry

        lax.fori_loop(1, TM, back, 0)
        pltpu.make_async_copy(
            t_out.at[tm], r_ref.at[SPACE_HEADS + tm // 2, :, pl.ds(HALF * lax.rem(tm, 2), HALF)], t_local_sem
        ).start()

    attend_unit(0)
    attend_temporal()

    def attend_later(unit, carry):
        attend_unit(unit)
        return carry

    lax.fori_loop(1, UNITS, attend_later, 0)

    def finish_unit(unit, carry):
        def one(step, inner):
            peer = space_peer(step)
            fwd_copy(unit, peer, space).wait_send()
            back_copy(unit, peer, space).wait_send()
            back_copy(unit, peer, peer).wait_recv()
            return inner

        lax.fori_loop(1, SPACE, one, 0)
        pltpu.make_async_copy(
            out_stage.at[unit, space], r_ref.at[2 * space + unit // 2, lax.rem(unit, 2)], local_sem.at[unit]
        ).wait()
        return carry

    lax.fori_loop(0, UNITS, finish_unit, 0)

    def finish_temporal(step, carry):
        peer = tm_peer(step)
        t_copy(peer, tm).wait_send()
        t_back_copy(peer, tm).wait_send()
        t_back_copy(peer, peer).wait_recv()
        return carry

    lax.fori_loop(1, TM, finish_temporal, 0)
    pltpu.make_async_copy(
        t_out.at[tm], r_ref.at[SPACE_HEADS + tm // 2, :, pl.ds(HALF * lax.rem(tm, 2), HALF)], t_local_sem
    ).wait()


def restore_kernel(inverse_ref, count_ref, r_ref, out_ref):
    first = lax.axis_index("tm") * FR
    for frame in range(FR):
        live = first + frame < count_ref[0]
        for head in range(HEADS):
            rows = r_ref[inverse_ref[head], frame]
            out_ref[frame, :, head * HD:(head + 1) * HD] = jnp.where(live, rows, jnp.zeros_like(rows))


def attend_call(order, frame_count, query, key_proj, value):
    block = (ROWS, HD)
    smem = pl.BlockSpec(memory_space=pltpu.SMEM)
    vmem = pl.BlockSpec(memory_space=pltpu.VMEM)
    return pl.pallas_call(
        attend_kernel,
        out_shape=jax.ShapeDtypeStruct((HEADS, FR) + block, jnp.bfloat16),
        in_specs=[smem, smem, vmem, vmem, vmem],
        out_specs=pl.BlockSpec(memory_space=pl.ANY),
        scratch_shapes=[
            pltpu.VMEM((UNITS, SPACE, 3) + block, jnp.bfloat16),
            pltpu.VMEM((UNITS, SPACE, 3) + block, jnp.bfloat16),
            pltpu.VMEM((TM, 3, FR, HALF, HD), jnp.bfloat16),
            pltpu.VMEM((TM, 3, FR, HALF, HD), jnp.bfloat16),
            pltpu.VMEM((UNITS, SPACE) + block, jnp.bfloat16),
            pltpu.VMEM((TM, FR, HALF, HD), jnp.bfloat16),
            pltpu.SemaphoreType.DMA((UNITS, SPACE)),
            pltpu.SemaphoreType.DMA((UNITS, SPACE)),
            pltpu.SemaphoreType.DMA((TM,)),
            pltpu.SemaphoreType.DMA((TM,)),
            pltpu.SemaphoreType.DMA((UNITS, SPACE)),
            pltpu.SemaphoreType.DMA((UNITS, SPACE)),
            pltpu.SemaphoreType.DMA((TM,)),
            pltpu.SemaphoreType.DMA((TM,)),
            pltpu.SemaphoreType.DMA((UNITS,)),
            pltpu.SemaphoreType.DMA,
        ],
        compiler_params=pltpu.CompilerParams(
            collective_id=0, has_side_effects=True, vmem_limit_bytes=52 * 2**20
        ),
        name="attend",
    )(order, frame_count, query, key_proj, value)


def restore_call(inverse, frame_count, results):
    step_rows = 64
    return pl.pallas_call(
        restore_kernel,
        out_shape=jax.ShapeDtypeStruct((FR, ROWS, HEADS * HD), jnp.bfloat16),
        grid=(ROWS // step_rows,),
        in_specs=[
            pl.BlockSpec(memory_space=pltpu.SMEM),
            pl.BlockSpec(memory_space=pltpu.SMEM),
            pl.BlockSpec((HEADS, FR, step_rows, HD), lambda i: (0, 0, i, 0)),
        ],
        out_specs=pl.BlockSpec((FR, step_rows, HEADS * HD), lambda i: (0, i, 0)),
        compiler_params=pltpu.CompilerParams(vmem_limit_bytes=16 * 2**20),
        name="restore",
    )(inverse, frame_count, results)


def on_device(query, key_proj, value, head_class, frame_count):
    heads = jnp.arange(HEADS, dtype=jnp.int32)
    earlier = heads[None, :] < heads[:, None]
    alike = head_class[None, :] == head_class[:, None]
    inverse = jnp.sum((earlier & alike).astype(jnp.int32), axis=1) + SPACE_HEADS * head_class
    order = jnp.sum(jnp.where(inverse[None, :] == heads[:, None], heads[None, :], 0), axis=1)
    results = attend_call(order, frame_count, query, key_proj, value)
    return restore_call(inverse, frame_count, results)


def solution(mesh):
    return jax.shard_map(
        on_device,
        mesh=mesh,
        in_specs=(P("tm", "space", None), P("tm", "space", None), P("tm", "space", None), P(), P()),
        out_specs=P("tm", "space", None),
        check_vma=False,
    )
```

time: 389 us -> 158 us (0.41)
  Pallas kernels: 0 us -> 154 us
  waiting for transfers between devices: 92.9 us -> 0 us
  local copies, waits for them, and re-layouts: 81.5 us -> 1.88 us
  matrix products: 64.5 us -> 0 us
  blocking collectives: 63.1 us -> 0 us
  other arithmetic: 59.3 us -> 1.69 us
  between operations: 14.2 us -> 0.67 us
  starting transfers between devices: 11.5 us -> 0 us
    pallas_call x0 -> x2, Pallas kernels: none -> 154 us  [the longest x1 150 us: attend_call(): pl.pallas_call(attend_kernel, out_shape=jax.ShapeDtypeStruct((HEADS, FR)...]
    dot_general x10 -> x0, matrix products: 64.5 us -> none  [the longest x1 19.3 us: temporal_folded(): jnp.einsum('fphd,gphd->fphg', query_time, key_piece, preferred_element_ty...]
    all_to_all x2 -> x0, blocking collectives: 63.1 us -> none  [the longest x1 33 us: on_device(): lax.all_to_all(values_space, 'space', split_axis=2, concat_axis=1, tiled=...]
    all_to_all x2 -> x0, waiting for transfers between devices: 55.7 us -> none  [the longest x1 27.9 us: on_device(): lax.all_to_all(query_space, 'space', split_axis=2, concat_axis=1, tiled=T...]
    reduce_sum x5 -> x2, other arithmetic: 42.3 us -> 1.03 us  [the longest x1 0.91 us: on_device(): jnp.sum((earlier & alike).astype(jnp.int32), axis=1)]
    all_gather x2 -> x0, waiting for transfers between devices: 37.2 us -> none  [the longest x1 37.2 us: temporal_folded(): value_piece = lax.all_gather(values_time, 'tm', axis=0, tiled=True)]
    gather x8 -> x0, local copies, waits for them, and re-layouts: 23.1 us -> none  [the longest x6 17.2 us: select(): jnp.take(array.reshape(frames_dev, pos_dev, HEADS, width // HEADS), chose...]
    unnamed x13 -> x2, local copies, waits for them, and re-layouts: 16.8 us -> 1.88 us
  transfers between devices with their start and end apart: 4 -> 0, of which waited for: 3 -> 0; matrix products, arithmetic and copies ran while one was open for 32% -> 0% of each run, Pallas kernels for 0% -> 0%
where the time goes in v1:
time: 158 us
  Pallas kernels  154 us (97%)
  local copies, waits for them, and re-layouts  1.88 us (1%)
  other arithmetic  1.69 us (1%)
    pallas_call x1, Pallas kernels, attend_call(): pl.pallas_call(attend_kernel, out_shape=jax.ShapeDtypeStruct((HEADS, FR)...  150 us

profile of v1, /device:TPU:1, one launch (start us, length us, event | category | flops | bytes accessed | tf_op | source)
XLA Modules:
  0.0 157.8 jit_solution(5659297828811940270)
XLA Ops:
  0.7 0.9 convert_reduce_fusion
  1.6 0.7 multiply_add_fusion.inverse_ref
  2.2 0.1 select_reduce_fusion.order_ref
  2.3 150.5 %attend.1.r_ref = bf16[24,2,256,128]{3,2,1,0:T(8,128)(2,1)} custom-call(s32[24]{0:T(128)S(1)} %select_reduce_fusion.order_ref, s32[1]{0:T(128)S(6)} %copy.6.count_ref, bf16[2,256,3072]{2,1,0:T(8,128)(2,1)} %q_ref.1, bf16[2,256,3072]{2,1,0:T(8,128)(2,1)} %k_ref.1, bf16[2,256,3072]{2,1,0:T(8,128)(2,1)} %v_ref.1), custom_call_target="tpu_custom_call" | custom-call | tf_op jit(solution)/shard_map/attend/pallas_call | solution.py:264
  152.8 0.0 copy-start
  152.9 1.9 %copy-done = bf16[24,2,256,128]{3,2,1,0:T(8,128)(2,1)S(1)} copy-done((bf16[24,2,256,128]{3,2,1,0:T(8,128)(2,1)S(1)}, bf16[24,2,256,128]{3,2,1,0:T(8,128)(2,1)}, u32[]{:S(2)}) %copy-start) | copy-done | bytes 3145752
  154.7 3.1 %restore.1 = bf16[2,256,3072]{2,1,0:T(8,128)(2,1)} custom-call(s32[24]{0:T(128)S(1)} %multiply_add_fusion.inverse_ref, s32[1]{0:T(128)S(6)} %copy.6.count_ref, bf16[24,2,256,128]{3,2,1,0:T(8,128)(2,1)S(1)} %copy-done), custom_call_target="tpu_custom_call" | custom-call | tf_op jit(solution)/shard_map/restore/pallas_call | solution.py:296
Async XLA Ops:
  152.8 1.9 %copy-start = (bf16[24,2,256,128]{3,2,1,0:T(8,128)(2,1)S(1)}, bf16[24,2,256,128]{3,2,1,0:T(8,128)(2,1)}, u32[]{:S(2)}) copy-start(bf16[24,2,256,128]{3,2,1,0:T(8,128)(2,1)} %attend.1.r_ref) | copy-start | bytes 9437188

commit v2 on v1

--- a/solution.py
+++ b/solution.py
@@ -18,6 +18,7 @@
 UNITS = 4
 HALF = ROWS // 2
 GROUP = 16
+STEP_ROWS = 64
 LOG2E = 1.4426950408889634
 EXP_SCALE = HD**-0.5 * LOG2E
 MASKED = -1e30
@@ -31,14 +32,32 @@
     return weights.astype(jnp.bfloat16), jnp.sum(weights, axis=-1, keepdims=True)
 
 
+def head_places(class_ref):
+    places, spatial, temporal = [], jnp.int32(0), jnp.int32(SPACE_HEADS)
+    for head in range(HEADS):
+        kind = class_ref[head]
+        places.append(jnp.where(kind == 0, spatial, temporal))
+        spatial = spatial + (1 - kind)
+        temporal = temporal + kind
+    return places
+
+
 def attend_kernel(
-    order_ref, count_ref, q_ref, k_ref, v_ref, r_ref,
-    stage, recv, t_stage, t_recv, out_stage, t_out,
+    class_ref, count_ref, q_ref, k_ref, v_ref, r_ref,
+    held_first, held_second, order_ref, load_sem, stage, recv, t_stage, t_recv, out_stage, t_out,
     fwd_send, fwd_recv, t_send, t_recv_sem, back_send, back_recv, tb_send, tb_recv, local_sem, t_local_sem,
 ):
     tm = lax.axis_index("tm")
     space = lax.axis_index("space")
     tensors = (q_ref, k_ref, v_ref)
+    held = (held_first, held_second)
+
+    def load_copy(frame, index):
+        return pltpu.make_async_copy(tensors[index].at[frame], held[frame].at[index], load_sem.at[frame, index])
+
+    for frame in range(FR):
+        for index in range(3):
+            load_copy(frame, index).start()
 
     def space_peer(step):
         return lax.rem(space // 2 + step // 2, 4) * 2 + lax.rem(space + step, 2)
@@ -92,14 +111,12 @@
     lax.fori_loop(1, TM, greet_tm, 0)
 
     def stage_unit(unit):
-        frame = lax.rem(unit, 2)
-
         def one(step, carry):
             peer = space_peer(step)
             head = order_ref[2 * peer + unit // 2]
             lanes = pl.ds(head * HD, HD)
-            for index, tensor in enumerate(tensors):
-                stage[unit, peer, index] = tensor[frame, :, lanes]
+            for index in range(3):
+                stage[unit, peer, index] = held[unit % 2][index, :, lanes]
             return carry
 
         lax.fori_loop(0, SPACE, one, 0)
@@ -117,9 +134,10 @@
         def one(step, carry):
             head = order_ref[SPACE_HEADS + step]
             lanes = pl.ds(head * HD, HD)
-            for index, tensor in enumerate(tensors):
+            for index in range(3):
                 for half in range(2):
-                    t_stage[2 * step + half, index] = tensor[:, half * HALF:(half + 1) * HALF, lanes]
+                    for frame in range(FR):
+                        t_stage[2 * step + half, index, frame] = held[frame][index, half * HALF:(half + 1) * HALF, lanes]
             return carry
 
         lax.fori_loop(0, TEMP_HEADS, one, 0)
@@ -132,18 +150,22 @@
         lax.fori_loop(1, TM, one, 0)
         t_recv[tm] = t_stage[tm]
 
+    places = head_places(class_ref)
+    for place in range(HEADS):
+        order_ref[place] = sum(jnp.where(places[head] == place, head, 0) for head in range(HEADS))
+    for index in range(3):
+        load_copy(0, index).wait()
     stage_unit(0)
     pl.semaphore_wait(barrier, SPACE + TM - 2)
     send_unit(0)
+    for index in range(3):
+        load_copy(1, index).wait()
     stage_temporal()
     send_temporal()
 
-    def later_unit(unit, carry):
+    for unit in range(1, UNITS):
         stage_unit(unit)
         send_unit(unit)
-        return carry
-
-    lax.fori_loop(1, UNITS, later_unit, 0)
 
     def attend_unit(unit):
         def arrived(step, carry):
@@ -248,25 +270,31 @@
     ).wait()
 
 
-def restore_kernel(inverse_ref, count_ref, r_ref, out_ref):
+def restore_kernel(class_ref, count_ref, r_ref, out_ref):
     first = lax.axis_index("tm") * FR
+    places = head_places(class_ref)
+    row = pl.multiple_of(pl.program_id(0) * STEP_ROWS, STEP_ROWS)
     for frame in range(FR):
         live = first + frame < count_ref[0]
         for head in range(HEADS):
-            rows = r_ref[inverse_ref[head], frame]
+            rows = r_ref[places[head], frame, pl.ds(row, STEP_ROWS)]
             out_ref[frame, :, head * HD:(head + 1) * HD] = jnp.where(live, rows, jnp.zeros_like(rows))
 
 
-def attend_call(order, frame_count, query, key_proj, value):
+def attend_call(head_class, frame_count, query, key_proj, value):
     block = (ROWS, HD)
     smem = pl.BlockSpec(memory_space=pltpu.SMEM)
-    vmem = pl.BlockSpec(memory_space=pltpu.VMEM)
+    hbm = pl.BlockSpec(memory_space=pltpu.HBM)
     return pl.pallas_call(
         attend_kernel,
-        out_shape=jax.ShapeDtypeStruct((HEADS, FR) + block, jnp.bfloat16),
-        in_specs=[smem, smem, vmem, vmem, vmem],
-        out_specs=pl.BlockSpec(memory_space=pl.ANY),
+        out_shape=pltpu.VMEM((HEADS, FR) + block, jnp.bfloat16),
+        in_specs=[smem, smem, hbm, hbm, hbm],
+        out_specs=pl.BlockSpec(memory_space=pltpu.VMEM),
         scratch_shapes=[
+            pltpu.VMEM((3, ROWS, HEADS * HD), jnp.bfloat16),
+            pltpu.VMEM((3, ROWS, HEADS * HD), jnp.bfloat16),
+            pltpu.SMEM((HEADS,), jnp.int32),
+            pltpu.SemaphoreType.DMA((FR, 3)),
             pltpu.VMEM((UNITS, SPACE, 3) + block, jnp.bfloat16),
             pltpu.VMEM((UNITS, SPACE, 3) + block, jnp.bfloat16),
             pltpu.VMEM((TM, 3, FR, HALF, HD), jnp.bfloat16),
@@ -288,34 +316,28 @@
             collective_id=0, has_side_effects=True, vmem_limit_bytes=52 * 2**20
         ),
         name="attend",
-    )(order, frame_count, query, key_proj, value)
-
-
-def restore_call(inverse, frame_count, results):
-    step_rows = 64
+    )(head_class, frame_count, query, key_proj, value)
+
+
+def restore_call(head_class, frame_count, results):
     return pl.pallas_call(
         restore_kernel,
         out_shape=jax.ShapeDtypeStruct((FR, ROWS, HEADS * HD), jnp.bfloat16),
-        grid=(ROWS // step_rows,),
+        grid=(ROWS // STEP_ROWS,),
         in_specs=[
             pl.BlockSpec(memory_space=pltpu.SMEM),
             pl.BlockSpec(memory_space=pltpu.SMEM),
-            pl.BlockSpec((HEADS, FR, step_rows, HD), lambda i: (0, 0, i, 0)),
+            pl.BlockSpec(memory_space=pltpu.VMEM),
         ],
-        out_specs=pl.BlockSpec((FR, step_rows, HEADS * HD), lambda i: (0, i, 0)),
+        out_specs=pl.BlockSpec((FR, STEP_ROWS, HEADS * HD), lambda i: (0, i, 0)),
         compiler_params=pltpu.CompilerParams(vmem_limit_bytes=16 * 2**20),
         name="restore",
-    )(inverse, frame_count, results)
+    )(head_class, frame_count, pltpu.with_memory_space_constraint(results, pltpu.VMEM))
 
 
 def on_device(query, key_proj, value, head_class, frame_count):
-    heads = jnp.arange(HEADS, dtype=jnp.int32)
-    earlier = heads[None, :] < heads[:, None]
-    alike = head_class[None, :] == head_class[:, None]
-    inverse = jnp.sum((earlier & alike).astype(jnp.int32), axis=1) + SPACE_HEADS * head_class
-    order = jnp.sum(jnp.where(inverse[None, :] == heads[:, None], heads[None, :], 0), axis=1)
-    results = attend_call(order, frame_count, query, key_proj, value)
-    return restore_call(inverse, frame_count, results)
+    results = attend_call(head_class, frame_count, query, key_proj, value)
+    return restore_call(head_class, frame_count, results)
 
 
 def solution(mesh):

time: 158 us -> 151 us (0.956)
  Pallas kernels: 154 us -> 150 us
  local copies, waits for them, and re-layouts: 1.88 us -> 0.01 us
  other arithmetic: 1.69 us -> 0 us
    pallas_call x1, Pallas kernels: 150 us -> 147 us  [attend_call(): pl.pallas_call(attend_kernel, out_shape=pltpu.VMEM((HEADS, FR) + block, j...]
    unnamed x2, local copies, waits for them, and re-layouts: 1.88 us -> 0.01 us
where the time goes in v2:
time: 151 us
  Pallas kernels  150 us (99%)
    pallas_call x1, Pallas kernels, attend_call(): pl.pallas_call(attend_kernel, out_shape=pltpu.VMEM((HEADS, FR) + block, j...  147 us
    pallas_call x1, Pallas kernels, restore_call(): pl.pallas_call(restore_kernel, out_shape=jax.ShapeDtypeStruct((FR, ROWS,...  3.03 us

profile of v2, /device:TPU:1, one launch (start us, length us, event | category | flops | bytes accessed | tf_op | source)
XLA Modules:
  0.0 151.1 jit_solution(8941648732646125962)
XLA Ops:
  0.7 0.0 copy-start
  0.7 147.4 %attend.1.r_ref = bf16[24,2,256,128]{3,2,1,0:T(8,128)(2,1)S(1)} custom-call(s32[24]{0:T(128)} %class_ref.3, s32[1]{0:T(128)S(6)} %copy.6.count_ref, bf16[2,256,3072]{2,1,0:T(8,128)(2,1)} %q_ref.1, bf16[2,256,3072]{2,1,0:T(8,128)(2,1)} %k_ref.1, bf16[2,256,3072]{2,1,0:T(8,128)(2,1)} %v_ref.1), custom_call_target="tpu_custom_call" | custom-call | tf_op jit(solution)/shard_map/attend/pallas_call | solution.py:288
  148.0 0.0 copy-done
  148.0 3.0 %restore.1 = bf16[2,256,3072]{2,1,0:T(8,128)(2,1)} custom-call(s32[24]{0:T(128)S(1)} %copy-done, s32[1]{0:T(128)S(6)} %copy.6.count_ref, bf16[24,2,256,128]{3,2,1,0:T(8,128)(2,1)S(1)} %attend.1.r_ref), custom_call_target="tpu_custom_call" | custom-call | tf_op jit(solution)/shard_map/restore/pallas_call | solution.py:323
Async XLA Ops:
  0.7 147.4 %copy-start = (s32[24]{0:T(128)S(1)}, s32[24]{0:T(128)}, u32[]{:S(2)}) copy-start(s32[24]{0:T(128)} %class_ref.3) | copy-start | bytes 292

commit v3 on v2

--- a/solution.py
+++ b/solution.py
@@ -18,7 +18,6 @@
 UNITS = 4
 HALF = ROWS // 2
 GROUP = 16
-STEP_ROWS = 64
 LOG2E = 1.4426950408889634
 EXP_SCALE = HD**-0.5 * LOG2E
 MASKED = -1e30
@@ -43,8 +42,8 @@
 
 
 def attend_kernel(
-    class_ref, count_ref, q_ref, k_ref, v_ref, r_ref,
-    held_first, held_second, order_ref, load_sem, stage, recv, t_stage, t_recv, out_stage, t_out,
+    class_ref, count_ref, q_ref, k_ref, v_ref, out_ref,
+    r_ref, held_first, held_second, order_ref, load_sem, stage, recv, t_stage, t_recv, out_stage, t_out,
     fwd_send, fwd_recv, t_send, t_recv_sem, back_send, back_recv, tb_send, tb_recv, local_sem, t_local_sem,
 ):
     tm = lax.axis_index("tm")
@@ -55,9 +54,8 @@
     def load_copy(frame, index):
         return pltpu.make_async_copy(tensors[index].at[frame], held[frame].at[index], load_sem.at[frame, index])
 
-    for frame in range(FR):
-        for index in range(3):
-            load_copy(frame, index).start()
+    for index in range(3):
+        load_copy(0, index).start()
 
     def space_peer(step):
         return lax.rem(space // 2 + step // 2, 4) * 2 + lax.rem(space + step, 2)
@@ -110,25 +108,21 @@
     lax.fori_loop(1, SPACE, greet_space, 0)
     lax.fori_loop(1, TM, greet_tm, 0)
 
-    def stage_unit(unit):
-        def one(step, carry):
-            peer = space_peer(step)
+    def send_unit(unit):
+        def pick(peer, refs):
             head = order_ref[2 * peer + unit // 2]
             lanes = pl.ds(head * HD, HD)
             for index in range(3):
-                stage[unit, peer, index] = held[unit % 2][index, :, lanes]
-            return carry
-
-        lax.fori_loop(0, SPACE, one, 0)
-
-    def send_unit(unit):
+                refs[index][...] = held[unit % 2][index, :, lanes]
+
         def one(step, carry):
             peer = space_peer(step)
+            pick(peer, [stage.at[unit, peer, index] for index in range(3)])
             fwd_copy(unit, peer, space).start()
             return carry
 
         lax.fori_loop(1, SPACE, one, 0)
-        recv[unit, space] = stage[unit, space]
+        pick(space, [recv.at[unit, space, index] for index in range(3)])
 
     def stage_temporal():
         def one(step, carry):
@@ -155,16 +149,15 @@
         order_ref[place] = sum(jnp.where(places[head] == place, head, 0) for head in range(HEADS))
     for index in range(3):
         load_copy(0, index).wait()
-    stage_unit(0)
+    for index in range(3):
+        load_copy(1, index).start()
     pl.semaphore_wait(barrier, SPACE + TM - 2)
     send_unit(0)
     for index in range(3):
         load_copy(1, index).wait()
     stage_temporal()
     send_temporal()
-
     for unit in range(1, UNITS):
-        stage_unit(unit)
         send_unit(unit)
 
     def attend_unit(unit):
@@ -269,16 +262,11 @@
         t_out.at[tm], r_ref.at[SPACE_HEADS + tm // 2, :, pl.ds(HALF * lax.rem(tm, 2), HALF)], t_local_sem
     ).wait()
 
-
-def restore_kernel(class_ref, count_ref, r_ref, out_ref):
-    first = lax.axis_index("tm") * FR
-    places = head_places(class_ref)
-    row = pl.multiple_of(pl.program_id(0) * STEP_ROWS, STEP_ROWS)
     for frame in range(FR):
-        live = first + frame < count_ref[0]
+        present = FR * tm + frame < count_ref[0]
         for head in range(HEADS):
-            rows = r_ref[places[head], frame, pl.ds(row, STEP_ROWS)]
-            out_ref[frame, :, head * HD:(head + 1) * HD] = jnp.where(live, rows, jnp.zeros_like(rows))
+            rows = r_ref[places[head], frame]
+            out_ref[frame, :, head * HD:(head + 1) * HD] = jnp.where(present, rows, jnp.zeros_like(rows))
 
 
 def attend_call(head_class, frame_count, query, key_proj, value):
@@ -287,10 +275,11 @@
     hbm = pl.BlockSpec(memory_space=pltpu.HBM)
     return pl.pallas_call(
         attend_kernel,
-        out_shape=pltpu.VMEM((HEADS, FR) + block, jnp.bfloat16),
+        out_shape=pltpu.VMEM((FR, ROWS, HEADS * HD), jnp.bfloat16),
         in_specs=[smem, smem, hbm, hbm, hbm],
         out_specs=pl.BlockSpec(memory_space=pltpu.VMEM),
         scratch_shapes=[
+            pltpu.VMEM((HEADS, FR) + block, jnp.bfloat16),
             pltpu.VMEM((3, ROWS, HEADS * HD), jnp.bfloat16),
             pltpu.VMEM((3, ROWS, HEADS * HD), jnp.bfloat16),
             pltpu.SMEM((HEADS,), jnp.int32),
@@ -319,25 +308,8 @@
     )(head_class, frame_count, query, key_proj, value)
 
 
-def restore_call(head_class, frame_count, results):
-    return pl.pallas_call(
-        restore_kernel,
-        out_shape=jax.ShapeDtypeStruct((FR, ROWS, HEADS * HD), jnp.bfloat16),
-        grid=(ROWS // STEP_ROWS,),
-        in_specs=[
-            pl.BlockSpec(memory_space=pltpu.SMEM),
-            pl.BlockSpec(memory_space=pltpu.SMEM),
-            pl.BlockSpec(memory_space=pltpu.VMEM),
-        ],
-        out_specs=pl.BlockSpec((FR, STEP_ROWS, HEADS * HD), lambda i: (0, i, 0)),
-        compiler_params=pltpu.CompilerParams(vmem_limit_bytes=16 * 2**20),
-        name="restore",
-    )(head_class, frame_count, pltpu.with_memory_space_constraint(results, pltpu.VMEM))
-
-
 def on_device(query, key_proj, value, head_class, frame_count):
-    results = attend_call(head_class, frame_count, query, key_proj, value)
-    return restore_call(head_class, frame_count, results)
+    return attend_call(head_class, frame_count, query, key_proj, value)
 
 
 def solution(mesh):

time: 151 us -> 151 us (level)
  Pallas kernels: 150 us -> 148 us
  local copies, waits for them, and re-layouts: 0.01 us -> 1.67 us
    pallas_call x2 -> x1, Pallas kernels: 150 us -> 148 us  [attend_call(): pl.pallas_call(attend_kernel, out_shape=pltpu.VMEM((FR, ROWS, HEADS * HD)...]
    unnamed x2 -> x1, local copies, waits for them, and re-layouts: 0.01 us -> 1.67 us
where the time goes in v3:
time: 151 us
  Pallas kernels  148 us (98%)
  local copies, waits for them, and re-layouts  1.67 us (1%)
    pallas_call x1, Pallas kernels, attend_call(): pl.pallas_call(attend_kernel, out_shape=pltpu.VMEM((FR, ROWS, HEADS * HD)...  148 us

profile of v3, /device:TPU:1, one launch (start us, length us, event | category | flops | bytes accessed | tf_op | source)
XLA Modules:
  0.0 150.6 jit_solution(3205683804768382049)
XLA Ops:
  0.7 148.3 %attend.1 = bf16[2,256,3072]{2,1,0:T(8,128)(2,1)S(1)} custom-call(s32[24]{0:T(128)} %class_ref.1, s32[1]{0:T(128)S(6)} %copy.8.count_ref, bf16[2,256,3072]{2,1,0:T(8,128)(2,1)} %q_ref.1, bf16[2,256,3072]{2,1,0:T(8,128)(2,1)} %k_ref.1, bf16[2,256,3072]{2,1,0:T(8,128)(2,1)} %v_ref.1), custom_call_target="tpu_custom_call" | custom-call | tf_op jit(solution)/shard_map/attend/pallas_call | solution.py:276
  149.0 1.7 %copy.7 = bf16[2,256,3072]{2,1,0:T(8,128)(2,1)} copy(bf16[2,256,3072]{2,1,0:T(8,128)(2,1)S(1)} %attend.1) | data formatting | bytes 6291456

commit v4 on v3

--- a/solution.py
+++ b/solution.py
@@ -18,6 +18,9 @@
 UNITS = 4
 HALF = ROWS // 2
 GROUP = 16
+HUB = SPACE - 1
+GATE = SPACE - 2
+UNIT_ORDER = (0, 2, 1, 3)
 LOG2E = 1.4426950408889634
 EXP_SCALE = HD**-0.5 * LOG2E
 MASKED = -1e30
@@ -45,6 +48,7 @@
     class_ref, count_ref, q_ref, k_ref, v_ref, out_ref,
     r_ref, held_first, held_second, order_ref, load_sem, stage, recv, t_stage, t_recv, out_stage, t_out,
     fwd_send, fwd_recv, t_send, t_recv_sem, back_send, back_recv, tb_send, tb_recv, local_sem, t_local_sem,
+    space_go, tm_go,
 ):
     tm = lax.axis_index("tm")
     space = lax.axis_index("space")
@@ -97,16 +101,42 @@
 
     barrier = pltpu.get_barrier_semaphore()
 
-    def greet_space(step, carry):
-        pl.semaphore_signal(barrier, inc=1, device_id=(tm, space_peer(step)), device_id_type=MESH)
-        return carry
-
-    def greet_tm(step, carry):
-        pl.semaphore_signal(barrier, inc=1, device_id=(tm_peer(step), space), device_id_type=MESH)
-        return carry
-
-    lax.fori_loop(1, SPACE, greet_space, 0)
-    lax.fori_loop(1, TM, greet_tm, 0)
+    def tell_space(sem, me):
+        for other in range(SPACE):
+            if other != me:
+                pl.semaphore_signal(sem, inc=1, device_id=(tm, other), device_id_type=MESH)
+
+    @pl.when(space != HUB)
+    def _():
+        pl.semaphore_signal(barrier, inc=1, device_id=(tm, HUB), device_id_type=MESH)
+
+    @pl.when(space == HUB)
+    def _():
+        pl.semaphore_wait(barrier, SPACE - 1)
+        tell_space(space_go, HUB)
+
+    def meet_space():
+        @pl.when(space != HUB)
+        def _():
+            pl.semaphore_wait(space_go, 1)
+
+        @pl.when(space == GATE)
+        def _():
+            def greet(step, carry):
+                pl.semaphore_signal(barrier, inc=1, device_id=(tm_peer(step), GATE), device_id_type=MESH)
+                return carry
+
+            lax.fori_loop(1, TM, greet, 0)
+
+    def meet_tm():
+        @pl.when(space == GATE)
+        def _():
+            pl.semaphore_wait(barrier, TM - 1)
+            tell_space(tm_go, GATE)
+
+        @pl.when(space != GATE)
+        def _():
+            pl.semaphore_wait(tm_go, 1)
 
     def send_unit(unit):
         def pick(peer, refs):
@@ -151,15 +181,7 @@
         load_copy(0, index).wait()
     for index in range(3):
         load_copy(1, index).start()
-    pl.semaphore_wait(barrier, SPACE + TM - 2)
-    send_unit(0)
-    for index in range(3):
-        load_copy(1, index).wait()
-    stage_temporal()
-    send_temporal()
-    for unit in range(1, UNITS):
-        send_unit(unit)
-
+    meet_space()
     def attend_unit(unit):
         def arrived(step, carry):
             peer = space_peer(step)
@@ -225,14 +247,21 @@
             t_out.at[tm], r_ref.at[SPACE_HEADS + tm // 2, :, pl.ds(HALF * lax.rem(tm, 2), HALF)], t_local_sem
         ).start()
 
-    attend_unit(0)
-    attend_temporal()
-
-    def attend_later(unit, carry):
+    def temporal_out():
+        for index in range(3):
+            load_copy(1, index).wait()
+        stage_temporal()
+        meet_tm()
+        send_temporal()
+
+    for place, unit in enumerate(UNIT_ORDER):
+        if place == 2:
+            temporal_out()
+        send_unit(unit)
+    for place, unit in enumerate(UNIT_ORDER):
+        if place == 1:
+            attend_temporal()
         attend_unit(unit)
-        return carry
-
-    lax.fori_loop(1, UNITS, attend_later, 0)
 
     def finish_unit(unit, carry):
         def one(step, inner):
@@ -300,6 +329,8 @@
             pltpu.SemaphoreType.DMA((TM,)),
             pltpu.SemaphoreType.DMA((UNITS,)),
             pltpu.SemaphoreType.DMA,
+            pltpu.SemaphoreType.REGULAR,
+            pltpu.SemaphoreType.REGULAR,
         ],
         compiler_params=pltpu.CompilerParams(
             collective_id=0, has_side_effects=True, vmem_limit_bytes=52 * 2**20

time: 151 us -> 150 us (level)
    pallas_call x1, Pallas kernels: 148 us -> 147 us  [attend_call(): pl.pallas_call(attend_kernel, out_shape=pltpu.VMEM((FR, ROWS, HEADS * HD)...]
where the time goes in v4:
time: 150 us; the launch traced here: 149 us
  Pallas kernels  147 us (98%)
  local copies, waits for them, and re-layouts  1.67 us (1%)
    pallas_call x1, Pallas kernels, attend_call(): pl.pallas_call(attend_kernel, out_shape=pltpu.VMEM((FR, ROWS, HEADS * HD)...  147 us

profile of v4, /device:TPU:1, one launch (start us, length us, event | category | flops | bytes accessed | tf_op | source)
XLA Modules:
  0.0 149.1 jit_solution(2211528383493745328)
XLA Ops:
  0.7 146.8 %attend.1 = bf16[2,256,3072]{2,1,0:T(8,128)(2,1)S(1)} custom-call(s32[24]{0:T(128)} %class_ref.1, s32[1]{0:T(128)S(6)} %copy.8.count_ref, bf16[2,256,3072]{2,1,0:T(8,128)(2,1)} %q_ref.1, bf16[2,256,3072]{2,1,0:T(8,128)(2,1)} %k_ref.1, bf16[2,256,3072]{2,1,0:T(8,128)(2,1)} %v_ref.1), custom_call_target="tpu_custom_call" | custom-call | tf_op jit(solution)/shard_map/attend/pallas_call | solution.py:305
  147.4 1.7 %copy.7 = bf16[2,256,3072]{2,1,0:T(8,128)(2,1)} copy(bf16[2,256,3072]{2,1,0:T(8,128)(2,1)S(1)} %attend.1) | data formatting | bytes 6291456

commit v5 on v4

--- a/solution.py
+++ b/solution.py
@@ -168,7 +168,7 @@
 
     def send_temporal():
         def one(step, carry):
-            t_copy(tm_peer(step), tm).start()
+            t_copy(tm_peer(TM - step), tm).start()
             return carry
 
         lax.fori_loop(1, TM, one, 0)
@@ -189,6 +189,7 @@
             return carry
 
         lax.fori_loop(1, SPACE, arrived, 0)
+        present = FR * tm + unit % FR < count_ref[0]
 
         def block(step, carry):
             peer = space_peer(lax.rem(step + 1, SPACE))
@@ -199,7 +200,7 @@
             )
             weights, total = softmax_parts(scores)
             mixed = jnp.dot(weights, values, preferred_element_type=jnp.float32)
-            out_stage[unit, peer] = (mixed / total).astype(jnp.bfloat16)
+            out_stage[unit, peer] = jnp.where(present, mixed / total, 0.0).astype(jnp.bfloat16)
 
             @pl.when(step < SPACE - 1)
             def _():
@@ -224,6 +225,7 @@
         column = lax.broadcasted_iota(jnp.int32, (width, width), 1)
         same = (row % GROUP) == (column % GROUP)
         allowed = same & (column < count_ref[0] * GROUP)
+        present = lax.broadcasted_iota(jnp.int32, (width, HD), 0) < count_ref[0] * GROUP
 
         def group(index, carry):
             span = pl.ds(pl.multiple_of(index * GROUP, GROUP), GROUP)
@@ -233,7 +235,8 @@
             scores = lax.dot_general(queries, keys, CONTRACT_LAST, preferred_element_type=jnp.float32)
             weights, total = softmax_parts(jnp.where(allowed, scores, MASKED))
             mixed = jnp.dot(weights, values, preferred_element_type=jnp.float32)
-            t_out[:, :, span] = (mixed / total).astype(jnp.bfloat16).reshape(TM, FR, GROUP, HD)
+            mixed = jnp.where(present, mixed / total, 0.0)
+            t_out[:, :, span] = mixed.astype(jnp.bfloat16).reshape(TM, FR, GROUP, HD)
             return carry
 
         lax.fori_loop(0, HALF // GROUP, group, 0)
@@ -292,10 +295,8 @@
     ).wait()
 
     for frame in range(FR):
-        present = FR * tm + frame < count_ref[0]
         for head in range(HEADS):
-            rows = r_ref[places[head], frame]
-            out_ref[frame, :, head * HD:(head + 1) * HD] = jnp.where(present, rows, jnp.zeros_like(rows))
+            out_ref[frame, :, head * HD:(head + 1) * HD] = r_ref[places[head], frame]
 
 
 def attend_call(head_class, frame_count, query, key_proj, value):

time: 150 us -> 148 us (0.987)
  Pallas kernels: 147 us -> 145 us
    pallas_call x1, Pallas kernels: 147 us -> 145 us  [attend_call(): pl.pallas_call(attend_kernel, out_shape=pltpu.VMEM((FR, ROWS, HEADS * HD)...]
where the time goes in v5:
time: 148 us; the launch traced here: 147 us
  Pallas kernels  145 us (98%)
  local copies, waits for them, and re-layouts  1.67 us (1%)
    pallas_call x1, Pallas kernels, attend_call(): pl.pallas_call(attend_kernel, out_shape=pltpu.VMEM((FR, ROWS, HEADS * HD)...  145 us

profile of v5, /device:TPU:1, one launch (start us, length us, event | category | flops | bytes accessed | tf_op | source)
XLA Modules:
  0.0 147.1 jit_solution(10111897646212865296)
XLA Ops:
  0.7 144.8 %attend.1 = bf16[2,256,3072]{2,1,0:T(8,128)(2,1)S(1)} custom-call(s32[24]{0:T(128)} %class_ref.1, s32[1]{0:T(128)S(6)} %copy.8.count_ref, bf16[2,256,3072]{2,1,0:T(8,128)(2,1)} %q_ref.1, bf16[2,256,3072]{2,1,0:T(8,128)(2,1)} %k_ref.1, bf16[2,256,3072]{2,1,0:T(8,128)(2,1)} %v_ref.1), custom_call_target="tpu_custom_call" | custom-call | tf_op jit(solution)/shard_map/attend/pallas_call | solution.py:306
  145.4 1.7 %copy.7 = bf16[2,256,3072]{2,1,0:T(8,128)(2,1)} copy(bf16[2,256,3072]{2,1,0:T(8,128)(2,1)S(1)} %attend.1) | data formatting | bytes 6291456

commit v6 on v5

--- a/solution.py
+++ b/solution.py
@@ -269,8 +269,6 @@
     def finish_unit(unit, carry):
         def one(step, inner):
             peer = space_peer(step)
-            fwd_copy(unit, peer, space).wait_send()
-            back_copy(unit, peer, space).wait_send()
             back_copy(unit, peer, peer).wait_recv()
             return inner
 
@@ -284,8 +282,6 @@
 
     def finish_temporal(step, carry):
         peer = tm_peer(step)
-        t_copy(peer, tm).wait_send()
-        t_back_copy(peer, tm).wait_send()
         t_back_copy(peer, peer).wait_recv()
         return carry
 
@@ -297,6 +293,22 @@
     for frame in range(FR):
         for head in range(HEADS):
             out_ref[frame, :, head * HD:(head + 1) * HD] = r_ref[places[head], frame]
+
+    def units_sent(step, carry):
+        peer = space_peer(step)
+        for unit in range(UNITS):
+            fwd_copy(unit, peer, space).wait_send()
+            back_copy(unit, peer, space).wait_send()
+        return carry
+
+    def temporal_sent(step, carry):
+        peer = tm_peer(step)
+        t_copy(peer, tm).wait_send()
+        t_back_copy(peer, tm).wait_send()
+        return carry
+
+    lax.fori_loop(1, SPACE, units_sent, 0)
+    lax.fori_loop(1, TM, temporal_sent, 0)
 
 
 def attend_call(head_class, frame_count, query, key_proj, value):

time: 148 us -> 148 us (level)
  no operation moved by 1% of the time
where the time goes in v6:
time: 148 us
  Pallas kernels  145 us (98%)
  local copies, waits for them, and re-layouts  1.67 us (1%)
    pallas_call x1, Pallas kernels, attend_call(): pl.pallas_call(attend_kernel, out_shape=pltpu.VMEM((FR, ROWS, HEADS * HD)...  145 us

profile of v6, /device:TPU:1, one launch (start us, length us, event | category | flops | bytes accessed | tf_op | source)
XLA Modules:
  0.0 147.6 jit_solution(16069112338967671584)
XLA Ops:
  0.7 145.2 %attend.1 = bf16[2,256,3072]{2,1,0:T(8,128)(2,1)S(1)} custom-call(s32[24]{0:T(128)} %class_ref.1, s32[1]{0:T(128)S(6)} %copy.8.count_ref, bf16[2,256,3072]{2,1,0:T(8,128)(2,1)} %q_ref.1, bf16[2,256,3072]{2,1,0:T(8,128)(2,1)} %k_ref.1, bf16[2,256,3072]{2,1,0:T(8,128)(2,1)} %v_ref.1), custom_call_target="tpu_custom_call" | custom-call | tf_op jit(solution)/shard_map/attend/pallas_call | solution.py:318
  145.9 1.7 %copy.7 = bf16[2,256,3072]{2,1,0:T(8,128)(2,1)} copy(bf16[2,256,3072]{2,1,0:T(8,128)(2,1)S(1)} %attend.1) | data formatting | bytes 6291456
